TPU v7x, 128 devices: a whole 4x4x4 slice. The times are simulated.
128 devices in a mesh: blk: 8 (over z, y_hi), tok: 16 (over x, y_lo, core).
Axes of the slice: x: 4, y: 4 (y_hi: 2, y_lo: 2; y = y_hi * 2 + y_lo), z: 4, core: 2. Of those that a mesh axis runs over, the one named last changes fastest.
Arguments:
- inputs: float32 [4096, 16384], P('tok', 'blk'), may hold values from -6 to 6
- first_factor: float32 [16, 1024, 1024], P('blk', 'tok'), may hold values from -0.1875 to 0.1875
- second_factor: float32 [16, 1024, 1024], P('blk', 'tok'), may hold values from -0.1875 to 0.1875
- cotangent: float32 [4096, 16384], P('tok', 'blk'), may hold values from -6 to 6
Outputs:
- input_grad: float32 [4096, 16384], P('tok', 'blk')
- first_grad: float32 [16, 1024, 1024], P('blk', 'tok')
- second_grad: float32 [16, 1024, 1024], P('blk', 'tok')
All inputs are finite; a program needn't handle non-finite values.
Results may differ from a plain program's by a relative error of at most 0.00013.
Values sent between devices are 32-bit elements; how exact they have to be, the bound alone decides.
A program may use at most 128 MiB of HBM per device.

v0:
```python
import math

import jax
import jax.numpy as jnp
from jax import lax
from jax.sharding import PartitionSpec as P


def body(inputs, first_factor, second_factor, cotangent):
    hp = lax.Precision.HIGHEST
    local_blocks = first_factor.shape[0]
    order = first_factor.shape[2]
    blocks = local_blocks * lax.axis_size("blk")
    group = order // blocks
    count = inputs.shape[0]
    xb = inputs.reshape(count, local_blocks, order)
    first_whole, second_whole = (
        lax.all_gather(first_factor, "tok", axis=1, tiled=True),
        lax.all_gather(second_factor, "tok", axis=1, tiled=True),
    )
    first_view = first_whole.reshape(local_blocks, order, blocks, group)
    first = jnp.einsum("tbi,bisg->stbg", xb, first_view, precision=hp).reshape(
        blocks, count, local_blocks * group
    )
    mixed = lax.all_to_all(first, "blk", split_axis=0, concat_axis=2, tiled=True)
    second = jnp.einsum("btk,bko->tbo", mixed, second_whole, precision=hp)
    normal_cdf = 0.5 * (1.0 + jax.scipy.special.erf(second / math.sqrt(2.0)))
    density = jnp.exp(-0.5 * second * second) / math.sqrt(2.0 * math.pi)
    delta_second = cotangent.reshape(count, local_blocks, order) * (normal_cdf + second * density)
    second_grad = jnp.einsum("btk,tbo->bko", mixed, delta_second, precision=hp)
    delta_mixed = jnp.einsum("tbo,bko->btk", delta_second, second_whole, precision=hp)
    delta_first = lax.all_to_all(delta_mixed, "blk", split_axis=2, concat_axis=0, tiled=True)
    delta_view = delta_first.reshape(blocks, count, local_blocks, group)
    first_grad = jnp.einsum("tbi,stbg->bisg", xb, delta_view, precision=hp).reshape(
        local_blocks, order, order
    )
    input_grad = jnp.einsum("stbg,bisg->tbi", delta_view, first_view, precision=hp).reshape(
        count, local_blocks * order
    )
    first_out, second_out = (
        lax.psum_scatter(first_grad, "tok", scatter_dimension=1, tiled=True),
        lax.psum_scatter(second_grad, "tok", scatter_dimension=1, tiled=True),
    )
    return (input_grad, first_out, second_out)


def solution(mesh):
    placed = (P("tok", "blk"), P("blk", "tok", None), P("blk", "tok", None), P("tok", "blk"))
    return jax.shard_map(
        body,
        mesh=mesh,
        in_specs=placed,
        out_specs=(P("tok", "blk"), P("blk", "tok", None), P("blk", "tok", None)),
        check_vma=False,
    )
```

profile of v0, /device:TPU:1, one launch (start us, length us, event | category | flops | bytes accessed | tf_op | source)
XLA Modules:
  0.0 388.7 jit_solution(9547876401872659460)
XLA Ops:
  7.2 0.7 all-gather.3.cloned.1.call-update
  7.9 0.7 all-gather.5.cloned.1.call-update
  8.6 3.0 reshape.30
  11.7 53.7 %all-gather.3.cloned.1.call-done = f32[2,1024,1024]{2,1,0:T(8,128)} async-done(((f32[2,64,1024]{2,1,0:T(8,128)}), f32[2,1024,1024]{2,1,0:T(8,128)}) %all-gather.3.cloned.1.call-update) | async-done | bytes 8388624 | tf_op jit(solution)/shard_map/all_gather | solution.py:18
  65.4 8.7 %copy.43 = f32[2,1024,1024]{1,2,0:T(8,128)} copy(f32[2,1024,1024]{2,1,0:T(8,128)} %all-gather.3.cloned.1.call-done) | data formatting | bytes 16777216 | tf_op jit(solution)/shard_map/all_gather | solution.py:18
  74.1 9.2 %fusion.15 = f32[16,256,2,64]{1,3,0,2:T(8,128)S(1)} fusion(f32[2,1024,16,64]{1,3,2,0:T(8,128)} %bitcast.43, f32[256,2,1024,1]{2,1,0,3:T(2,128)S(1)} %bitcast.46), kind=kOutput, calls=%fused_computation.17 | convolution fusion | flops 6442450944 | bytes 12582912 | tf_op jit(solution)/shard_map/tbi,bisg->stbg/dot_general | solution.py:22
  83.3 1.5 copy.45
  84.8 6.5 %all-to-all-start = ((f32[16,256,128]{1,2,0:T(8,128)}), f32[16,256,128]{1,2,0:T(8,128)S(1)}, u32[]{:S(2)}, u32[]{:S(2)}) async-start(f32[16,256,128]{1,2,0:T(8,128)} %bitcast.49), calls=%async_computation | async-start | bytes 4194304 | tf_op jit(solution)/shard_map/all_to_all | solution.py:25
  91.3 0.2 reduce-scatter.5.cloned.1.call-start
  91.5 2.9 copy.42
  94.5 2.9 copy.48
  97.4 45.0 %all-to-all-done = f32[16,256,128]{1,2,0:T(8,128)S(1)} async-done(((f32[16,256,128]{1,2,0:T(8,128)}), f32[16,256,128]{1,2,0:T(8,128)S(1)}, u32[]{:S(2)}, u32[]{:S(2)}) %all-to-all-start) | async-done | bytes 2097184 | tf_op jit(solution)/shard_map/all_to_all | solution.py:25
  142.4 1.8 copy.47
  144.2 1.7 all_to_all.27
  146.0 10.3 %fusion.6 = f32[256,2,1024]{2,0,1:T(8,128)S(1)} fusion(f32[256,2,1024]{2,0,1:T(8,128)} %copy.48, f32[2,256,1024]{2,1,0:T(8,128)S(1)} %all_to_all.27, f32[2,1024,1024]{2,1,0:T(8,128)} %all-gather.5.cloned.1.call-done), kind=kOutput, calls=%fused_computation.7 | convolution fusion | flops 6447169536 | bytes 14680064 | tf_op jit(solution)/shard_map/btk,bko->tbo/dot_general | solution.py:26
  156.3 1.3 copy-done
  157.6 9.0 %fusion.22 = f32[2,1024,1024]{2,1,0:T(8,128)} fusion(f32[2,256,1024]{2,1,0:T(8,128)S(1)} %all_to_all.27, f32[256,2,1024]{2,0,1:T(8,128)S(1)} %fusion.6), kind=kOutput, calls=%fused_computation.20 | convolution fusion | flops 6442450944 | bytes 12582912 | tf_op jit(solution)/shard_map/btk,tbo->bko/dot_general | solution.py:30
  166.6 0.0 reduce-scatter.3.cloned.1.call-start
  166.6 1.5 copy-done.1
  168.1 10.6 %fusion.21 = f32[2,256,1024]{2,1,0:T(8,128)} fusion(f32[256,2,1024]{2,0,1:T(8,128)S(1)} %copy-done.1, f32[2,1024,1024]{2,1,0:T(8,128)} %all-gather.5.cloned.1.call-done), kind=kOutput, calls=%fused_computation.19 | convolution fusion | flops 6442450944 | bytes 12582912 | tf_op jit(solution)/shard_map/tbo,bko->btk/dot_general | solution.py:31
  178.7 2.8 copy.49
  181.6 52.0 %all_to_all.33 = f32[2,256,1024]{1,0,2:T(2,128)S(1)} all-to-all(f32[2,256,1024]{1,0,2:T(2,128)S(1)} %copy.49), channel_id=1, replica_groups=mesh['blk'=8,'tok'=16] {'blk'}, dimensions={2} | all-to-all | bytes 4194304 | tf_op jit(solution)/shard_map/all_to_all | solution.py:32
  233.6 0.2 copy.50
  233.8 0.1 copy.51
  233.9 1.5 copy-done.3
  235.4 9.2 %fusion.10 = f32[2,16,64,1024]{3,2,1,0:T(8,128)} fusion(f32[16,256,2,64]{1,3,2,0:T(8,128)S(1)} %bitcast.53, f32[256,2,1024,1]{2,1,0,3:T(2,128)S(1)} %bitcast.47), kind=kOutput, calls=%fused_computation.12 | convolution fusion | flops 6442450944 | bytes 12582912 | tf_op jit(solution)/shard_map/tbi,stbg->bisg/dot_general | solution.py:34
  244.5 8.7 %copy.56 = f32[2,1024,1024]{2,1,0:T(8,128)} copy(f32[2,1024,1024]{1,2,0:T(8,128)} %bitcast.45) | data formatting | bytes 16777216 | tf_op jit(solution)/shard_map/reshape | solution.py:34
  253.3 10.5 %fusion.18 = f32[256,2,1024]{2,0,1:T(8,128)} fusion(f32[16,256,2,64]{1,3,2,0:T(8,128)S(1)} %bitcast.54, f32[2,1024,16,64]{1,3,2,0:T(8,128)} %bitcast.44), kind=kOutput, calls=%fused_computation.18 | convolution fusion | flops 6442450944 | bytes 12582912 | tf_op jit(solution)/shard_map/stbg,bisg->tbi/dot_general | solution.py:37
  263.8 1.9 copy.53
  265.7 1.8 copy.58
  267.6 15.3 %reduce-scatter.5.cloned.1.call-done = f32[2,64,1024]{2,1,0:T(8,128)} async-done(((f32[2,1024,1024]{2,1,0:T(8,128)}), f32[2,64,1024]{2,1,0:T(8,128)}) %reduce-scatter.5.cloned.1.call-update) | async-done | bytes 524304 | tf_op jit(solution)/shard_map/reduce_scatter | solution.py:42
  282.9 99.3 %reduce-scatter.3.cloned.1.call-done = f32[2,64,1024]{2,1,0:T(8,128)} async-done(((f32[2,1024,1024]{2,1,0:T(8,128)}), f32[2,64,1024]{2,1,0:T(8,128)}) %reduce-scatter.3.cloned.1.call-update) | async-done | bytes 524304 | tf_op jit(solution)/shard_map/reduce_scatter | solution.py:41
  (10 shorter events, 0.1 us)
Async XLA Ops:
  7.2 58.3 %all-gather.3.cloned.1.call-start = ((), (), s32[]{:S(2)}) async-start(), calls=%async_computation.4 | async-start | bytes 8912896 | tf_op jit(solution)/shard_map/all_gather | solution.py:18
  7.9 138.1 %all-gather.5.cloned.1.call-start = ((), (), s32[]{:S(2)}) async-start(), calls=%async_computation.5 | async-start | bytes 8912896 | tf_op jit(solution)/shard_map/all_gather | solution.py:19
  11.7 62.4 %copy-start.2 = (f32[256,2,1024]{2,1,0:T(2,128)}, f32[256,2,1024]{2,1,0:T(2,128)S(1)}, u32[]{:S(2)}) copy-start(f32[256,2,1024]{2,1,0:T(2,128)S(1)} %reshape.30) | copy-start | bytes 6291460
  84.8 57.6 %all-to-all-start = ((f32[16,256,128]{1,2,0:T(8,128)}), f32[16,256,128]{1,2,0:T(8,128)S(1)}, u32[]{:S(2)}, u32[]{:S(2)}) async-start(f32[16,256,128]{1,2,0:T(8,128)} %bitcast.49), calls=%async_computation | async-start | bytes 4194304 | tf_op jit(solution)/shard_map/all_to_all | solution.py:25
  91.3 191.6 %reduce-scatter.5.cloned.1.call-start = ((), (), s32[]{:S(2)}) async-start(), calls=%async_computation.7 | async-start | bytes 8912896 | tf_op jit(solution)/shard_map/reduce_scatter | solution.py:42
  156.3 1.3 copy-start
  166.5 1.6 copy-start.1
  166.6 215.6 %reduce-scatter.3.cloned.1.call-start = ((), (), s32[]{:S(2)}) async-start(), calls=%async_computation.6 | async-start | bytes 8912896 | tf_op jit(solution)/shard_map/reduce_scatter | solution.py:41
  233.7 1.6 copy-start.3
Sparse Core Ops, SparseCore 0:
  9.7 55.7 all-gather.2
  67.1 75.4 all-gather.4
  166.7 116.1 reduce-scatter.4
  285.7 96.3 reduce-scatter.2
where the time goes:
time: 390 us; the launch traced here: 389 us
  waiting for transfers between devices  215 us (55%)
  matrix products  58.6 us (15%)
  blocking collectives  52 us (13%)
  local copies, waits for them, and re-layouts  42.6 us (11%)
  between operations  13.9 us (4%)
  starting transfers between devices  6.81 us (2%)
    reduce_scatter x1, waiting for transfers between devices, body(): lax.psum_scatter(first_grad, 'tok', scatter_dimension=1, tiled=True)  99.3 us
    all_gather x1, waiting for transfers between devices, body(): lax.all_gather(first_factor, 'tok', axis=1, tiled=True)  53.7 us
    all_to_all x1, blocking collectives, body(): lax.all_to_all(delta_mixed, 'blk', split_axis=2, concat_axis=0, tiled=True)  52 us
    all_to_all x1, waiting for transfers between devices, body(): lax.all_to_all(first, 'blk', split_axis=0, concat_axis=2, tiled=True)  45 us
    reduce_scatter x1, waiting for transfers between devices, body(): lax.psum_scatter(second_grad, 'tok', scatter_dimension=1, tiled=True)  15.3 us
    dot_general x1, matrix products, body(): jnp.einsum('tbo,bko->btk', delta_second, second_whole, precision=hp)  10.6 us
    dot_general x1, matrix products, body(): jnp.einsum('stbg,bisg->tbi', delta_view, first_view, precision=hp)  10.5 us
    dot_general x1, matrix products, body(): second = jnp.einsum('btk,bko->tbo', mixed, second_whole, precision=hp)  10.3 us
  transfers between devices with their start and end apart: 5, of which 4 were waited for; matrix products, arithmetic and copies ran while one was open for 20% of the time, Pallas kernels for 0%

commit v1 on v0

v1 whole, which is shorter than its diff:
```python
import math

import jax
import jax.numpy as jnp
from jax import lax
from jax.experimental import pallas as pl
from jax.experimental.pallas import tpu as pltpu
from jax.sharding import PartitionSpec as P

F32 = jnp.float32
BF16 = jnp.bfloat16
XS = 4
NN = (((1,), (0,)), ((), ()))
NT = (((1,), (1,)), ((), ()))
AG_OVER_Y = (True, False)
RS_OVER_Y = (True, False)


def halves(v):
    high = v.astype(BF16)
    return high, (v - high.astype(F32)).astype(BF16)


def product(ah, al, bh, bl, dims):
    def dot(a, b):
        return lax.dot_general(a, b, dims, preferred_element_type=F32)

    return dot(ah, bh) + (dot(ah, bl) + dot(al, bh))


def rows_at(index, size):
    return pl.ds(pl.multiple_of(index * size, size), size)


def kernel(
    x_hbm, w1_hbm, w2_hbm, cot_hbm, dx_hbm, g1_hbm, g2_hbm,
    wbuf, wh, wl, xs, cs, ah, al, xth, xtl, ft, mt, mth, mtl, d2h, d2l, dmt, d1t, rbuf,
    loc_sem, pair_send, pair_recv, ag_send, ag_recv, a2a_send, a2a_recv, rs_send, rs_recv,
):
    w_hbm = (w1_hbm, w2_hbm)
    g_hbm = (g1_hbm, g2_hbm)
    k = lax.axis_index("blk")
    t = lax.axis_index("tok")
    x = t // 4
    y = (t // 2) % 2
    c = t % 2
    oc = 1 - c
    count = x_hbm.shape[0]
    slab = w1_hbm.shape[1]
    order = w1_hbm.shape[2]
    chip = 2 * count
    group = order // 16

    def tok(dx, other_y, core):
        yy = 1 - y if other_y else y
        return {"tok": ((x + dx) % XS) * 4 + yy * 2 + core}

    def slab_of(dx, other_y, core):
        return tok(dx, other_y, core)["tok"]

    def remote(src, dst, send, recv, to):
        return pltpu.make_async_remote_copy(
            src_ref=src, dst_ref=dst, send_sem=send, recv_sem=recv, device_id=to, device_id_type=pl.DeviceIdType.MESH
        )

    mine = rows_at(c, order)
    theirs = rows_at(oc, order)
    own = rows_at(c, count)
    local = [
        pltpu.make_async_copy(x_hbm.at[:, mine], xs.at[own], loc_sem.at[0]),
        pltpu.make_async_copy(cot_hbm.at[:, mine], cs.at[own], loc_sem.at[1]),
        pltpu.make_async_copy(w1_hbm.at[c], wbuf.at[0, rows_at(t, slab)], loc_sem.at[2]),
        pltpu.make_async_copy(w2_hbm.at[c], wbuf.at[1, rows_at(t, slab)], loc_sem.at[3]),
    ]
    for cp in local:
        cp.start()

    barrier = pltpu.get_barrier_semaphore()
    near = [tok(1, False, c), tok(-1 + XS, False, c), tok(0, True, c), tok(0, False, oc)]
    near += [tok(1, False, oc), tok(-1 + XS, False, oc), tok(0, True, oc)]
    for to in near:
        pl.semaphore_signal(barrier, inc=1, device_id=to, device_id_type=pl.DeviceIdType.MESH)

    def greet(i, _):
        kk = (k + 1 + i // 2) % 8
        pl.semaphore_signal(
            barrier, inc=1, device_id={"blk": kk, "tok": t - c + i % 2}, device_id_type=pl.DeviceIdType.MESH
        )
        return 0

    lax.fori_loop(0, 14, greet, 0)
    pl.semaphore_wait(barrier, 14 + len(near))

    def ag(f, n, src, row, to):
        return remote(src, wbuf.at[f, rows_at(row, slab)], ag_send.at[f, n], ag_recv.at[f, row], to)

    def forward(f, n, row, to):
        cp = ag(f, n, wbuf.at[f, rows_at(row, slab)], row, to)
        cp.start()

    def ag_first(f):
        for h in range(2):
            ag(f, h, w_hbm[f].at[h], t, tok(1, False, h)).start()
            ag(f, 2 + h, w_hbm[f].at[h], t, tok(XS - 1, False, h)).start()
            ag(f, 4 + h, w_hbm[f].at[h], t, tok(0, True, h)).start()
        ag(f, 6, w_hbm[f].at[oc], t, tok(0, False, oc)).start()

    def ag_wait(f, row):
        ag(f, 0, wbuf.at[f, rows_at(row, slab)], row, tok(1, False, c)).wait_recv()

    def ag_second(f):
        low, high = slab_of(XS - 1, False, 0), slab_of(1, False, 1)
        ag_wait(f, low)
        forward(f, 7, low, tok(1, False, c))
        ag_wait(f, high)
        forward(f, 8, high, tok(XS - 1, False, c))
        for h in range(2):
            row = slab_of(0, True, h)
            ag_wait(f, row)
            forward(f, 9 + h, row, tok(1, False, c))
            forward(f, 11 + h, row, tok(XS - 1, False, c))

    def ag_third(f):
        if AG_OVER_Y[f]:
            for h in range(2):
                row = slab_of(2, False, h)
                ag_wait(f, row)
                forward(f, 13 + h, row, tok(0, True, c))
        else:
            low, high = slab_of(XS - 1, True, 0), slab_of(1, True, 1)
            ag_wait(f, low)
            forward(f, 13, low, tok(1, False, c))
            ag_wait(f, high)
            forward(f, 14, high, tok(XS - 1, False, c))

    def ag_rest(f):
        ag_wait(f, slab_of(0, False, oc))
        ag_wait(f, slab_of(XS - 1, False, 1))
        ag_wait(f, slab_of(1, False, 0))
        if AG_OVER_Y[f]:
            for h in range(2):
                ag_wait(f, slab_of(1, True, h))
                ag_wait(f, slab_of(XS - 1, True, h))
        else:
            for h in range(2):
                ag_wait(f, slab_of(2, False, h))
            ag_wait(f, slab_of(XS - 1, True, 1))
            ag_wait(f, slab_of(1, True, 0))
        for h in range(2):
            ag_wait(f, slab_of(2, True, h))

    def ag_sent(f):
        for n in range(15):
            ag(f, n, wbuf.at[f, rows_at(t, slab)], t, tok(1, False, c)).wait_send()

    def split_factor(f):
        def step(i, _):
            at = rows_at(i, 128)
            high, low = halves(wbuf[f, at, :])
            wh[f, at, :] = high
            wl[f, at, :] = low
            return 0

        lax.fori_loop(0, order // 128, step, 0)

    ag_first(0)
    pair = tok(0, False, oc)
    swap = [
        remote(x_hbm.at[:, theirs], xs.at[own], pair_send.at[0], pair_recv.at[0], pair),
        remote(cot_hbm.at[:, theirs], cs.at[own], pair_send.at[1], pair_recv.at[1], pair),
    ]
    for cp in swap:
        cp.start()
    for cp in local:
        cp.wait()
    for cp in swap:
        cp.wait()

    def split_x(i, _):
        at = rows_at(i, 128)
        high, low = halves(xs[:, at])
        ah[:, at] = high
        al[:, at] = low
        high, low = halves(xs[:, at].T)
        xth[at, :] = high
        xtl[at, :] = low
        return 0

    lax.fori_loop(0, order // 128, split_x, 0)

    ag_second(0)
    ag_third(0)
    ag_first(1)
    ag_rest(0)
    split_factor(0)

    me = 2 * k + c
    base = t - c

    def a2a(n, src, dst, s):
        return remote(
            src.at[rows_at(s, group)], dst.at[rows_at(me, group)], a2a_send.at[n, s], a2a_recv.at[n, me],
            {"blk": s // 2, "tok": base + s % 2},
        )

    def a2a_start(n, src, dst, s):
        @pl.when(s != me)
        def _():
            a2a(n, src, dst, s).start()

        @pl.when(s == me)
        def _():
            dst[rows_at(me, group), :] = src[rows_at(me, group), :]

    def a2a_wait(n, src, dst):
        def step(s, _):
            @pl.when(s != me)
            def _():
                remote(
                    src.at[rows_at(s, group)], dst.at[rows_at(s, group)], a2a_send.at[n, s], a2a_recv.at[n, s],
                    {"blk": s // 2, "tok": base + s % 2},
                ).wait_recv()

            return 0

        lax.fori_loop(0, 16, step, 0)

    def a2a_sent(n, src, dst):
        def step(s, _):
            @pl.when(s != me)
            def _():
                a2a(n, src, dst, s).wait_send()

            return 0

        lax.fori_loop(0, 16, step, 0)

    z = k // 2

    def first_step(i, _):
        q = (z + 1 + i) % 4
        at = rows_at(q, 256)
        part = product(ah[...], al[...], wh[0, :, at], wl[0, :, at], NN)
        ft[at, :] = part.T
        for r in range(4):
            a2a_start(0, ft, mt, 4 * q + r)
        return 0

    lax.fori_loop(0, 4, first_step, 0)

    ag_second(1)
    ag_third(1)
    ag_rest(1)
    split_factor(1)
    a2a_wait(0, ft, mt)

    def turn(src, keep):
        def step(i, _):
            at = rows_at(i, 128)
            v = src[at, :]
            if keep:
                high, low = halves(v)
                mth[at, :] = high
                mtl[at, :] = low
            high, low = halves(v.T)
            ah[:, at] = high
            al[:, at] = low
            return 0

        lax.fori_loop(0, order // 128, step, 0)

    turn(mt, True)

    def second_step(i, _):
        at = rows_at(i, 256)
        v = product(ah[...], al[...], wh[1, :, at], wl[1, :, at], NN)
        cdf = 0.5 * (1.0 + lax.erf(v * (1.0 / math.sqrt(2.0))))
        density = jnp.exp(-0.5 * v * v) * (1.0 / math.sqrt(2.0 * math.pi))
        high, low = halves(cs[:, at] * (cdf + v * density))
        d2h[:, at] = high
        d2l[:, at] = low
        return 0

    lax.fori_loop(0, 4, second_step, 0)

    def mixed_step(i, _):
        q = (z + 1 + i) % 4
        at = rows_at(q, 256)
        dmt[at, :] = product(wh[1, at, :], wl[1, at, :], d2h[...], d2l[...], NT)
        for r in range(4):
            a2a_start(1, dmt, d1t, 4 * q + r)
        return 0

    lax.fori_loop(0, 4, mixed_step, 0)

    def rs(f, slot, row, to):
        return remote(
            wbuf.at[f, rows_at(row, slab)], rbuf.at[f, slot], rs_send.at[f, slot], rs_recv.at[f, slot], to
        )

    def rs_start(f, slot, row):
        if slot in (1, 2, 3, 7, 8, 9) and not (RS_OVER_Y[f] and slot == 1):
            to = tok(1, False, c)
        elif slot in (0, 1, 12, 13) and (RS_OVER_Y[f] or slot >= 12):
            to = tok(0, True, c)
        else:
            to = tok(XS - 1, False, c)
        rs(f, slot, row, to).start()

    def rs_add(f, row, slots):
        for slot in slots:
            rs(f, slot, t, tok(1, False, c)).wait_recv()
        at = rows_at(row, slab)
        total = rbuf[f, slots[0]]
        for slot in slots[1:]:
            total = total + rbuf[f, slot]
        wbuf[f, at, :] = wbuf[f, at, :] + total

    def gradient(f, lh, ll, rh, rl):
        for dx in (2, 1, 3, 0):
            at = rows_at((x + dx) % XS, 256)
            wbuf[f, at, :] = product(lh[at, :], ll[at, :], rh[...], rl[...], NN)
            if dx == 2:
                if RS_OVER_Y[f]:
                    rs_start(f, 0, slab_of(2, True, 0))
                    rs_start(f, 1, slab_of(2, True, 1))
                else:
                    rs_start(f, 6, slab_of(2, False, 0))
                    rs_start(f, 7, slab_of(2, False, 1))
                    rs_start(f, 0, slab_of(2, True, 0))
                    rs_start(f, 1, slab_of(2, True, 1))
            elif dx == 1:
                rs_start(f, 2, slab_of(1, True, 0))
                if RS_OVER_Y[f]:
                    rs_start(f, 3, slab_of(1, True, 1))
                rs_start(f, 8, slab_of(1, False, 0))
            elif dx == 3:
                rs_start(f, 5, slab_of(3, True, 1))
                if RS_OVER_Y[f]:
                    rs_start(f, 4, slab_of(3, True, 0))
                rs_start(f, 11, slab_of(3, False, 1))

    def rs_middle(f):
        if RS_OVER_Y[f]:
            for h in range(2):
                row = slab_of(2, False, h)
                rs_add(f, row, (h,))
                rs_start(f, 6 + h, row)
        else:
            row = slab_of(1, True, 1)
            rs_add(f, row, (1,))
            rs_start(f, 3, row)
            row = slab_of(3, True, 0)
            rs_add(f, row, (0,))
            rs_start(f, 4, row)
        row = slab_of(1, False, 1)
        rs_add(f, row, (7,))
        rs_start(f, 9, row)
        row = slab_of(3, False, 0)
        rs_add(f, row, (6,))
        rs_start(f, 10, row)
        for h in range(2):
            row = slab_of(0, True, h)
            rs_add(f, row, (2 + h, 4 + h))
            rs_start(f, 12 + h, row)

    def out_local(f):
        return pltpu.make_async_copy(wbuf.at[f, rows_at(t, slab)], g_hbm[f].at[c], loc_sem.at[f])

    def out_pair(f):
        return remote(
            wbuf.at[f, rows_at(base + oc, slab)], g_hbm[f].at[c], rs_send.at[f, 14], rs_recv.at[f, 14], pair
        )

    def out_wait(f):
        return remote(
            wbuf.at[f, rows_at(base + oc, slab)], g_hbm[f].at[oc], rs_send.at[f, 14], rs_recv.at[f, 14], pair
        )

    def rs_end(f):
        for h in range(2):
            rs_add(f, slab_of(0, False, h), (8 + h, 10 + h, 12 + h))
        out_pair(f).start()
        out_local(f).start()

    def rs_done(f):
        out_local(f).wait()
        out_pair(f).wait_send()
        out_wait(f).wait_recv()
        for slot in range(14):
            rs(f, slot, t, tok(1, False, c)).wait_send()

    ag_sent(1)
    gradient(1, mth, mtl, d2h, d2l)
    rs_middle(1)
    a2a_wait(1, dmt, d1t)
    turn(d1t, False)
    ag_sent(0)
    gradient(0, xth, xtl, ah, al)

    def input_step(i, _):
        at = rows_at(i, 256)
        xs[:, at] = product(ah[...], al[...], wh[0, at, :], wl[0, at, :], NT)
        return 0

    lax.fori_loop(0, 4, input_step, 0)
    dx_pair = remote(xs.at[rows_at(oc, count)], dx_hbm.at[:, mine], pair_send.at[2], pair_recv.at[2], pair)
    dx_wait = remote(xs.at[rows_at(oc, count)], dx_hbm.at[:, theirs], pair_send.at[2], pair_recv.at[2], pair)
    dx_local = pltpu.make_async_copy(xs.at[own], dx_hbm.at[:, mine], loc_sem.at[2])
    dx_pair.start()
    dx_local.start()
    rs_end(1)
    rs_middle(0)
    rs_end(0)
    dx_local.wait()
    dx_pair.wait_send()
    dx_wait.wait_recv()
    a2a_sent(0, ft, mt)
    a2a_sent(1, dmt, d1t)
    rs_done(1)
    rs_done(0)


def body(inputs, first_factor, second_factor, cotangent):
    count, width = inputs.shape
    blocks, slab, order = first_factor.shape
    chip = 2 * count
    wide = (chip, order)
    tall = (order, chip)
    dma = pltpu.SemaphoreType.DMA
    return pl.pallas_call(
        kernel,
        out_shape=(
            jax.ShapeDtypeStruct((count, width), F32),
            jax.ShapeDtypeStruct((blocks, slab, order), F32),
            jax.ShapeDtypeStruct((blocks, slab, order), F32),
        ),
        in_specs=[pl.BlockSpec(memory_space=pl.ANY)] * 4,
        out_specs=[pl.BlockSpec(memory_space=pl.ANY)] * 3,
        scratch_shapes=[
            pltpu.VMEM((2, order, order), F32),
            pltpu.VMEM((2, order, order), BF16),
            pltpu.VMEM((2, order, order), BF16),
            pltpu.VMEM(wide, F32),
            pltpu.VMEM(wide, F32),
            pltpu.VMEM(wide, BF16),
            pltpu.VMEM(wide, BF16),
            pltpu.VMEM(tall, BF16),
            pltpu.VMEM(tall, BF16),
            pltpu.VMEM(tall, F32),
            pltpu.VMEM(tall, F32),
            pltpu.VMEM(tall, BF16),
            pltpu.VMEM(tall, BF16),
            pltpu.VMEM(wide, BF16),
            pltpu.VMEM(wide, BF16),
            pltpu.VMEM(tall, F32),
            pltpu.VMEM(tall, F32),
            pltpu.VMEM((2, 14, slab, order), F32),
            dma((4,)),
            dma((3,)),
            dma((3,)),
            dma((2, 15)),
            dma((2, 16)),
            dma((2, 16)),
            dma((2, 16)),
            dma((2, 15)),
            dma((2, 15)),
        ],
        compiler_params=pltpu.CompilerParams(
            collective_id=0, has_side_effects=True, vmem_limit_bytes=60 * 1024 * 1024
        ),
        cost_estimate=pl.CostEstimate(flops=19 * 10**9, bytes_accessed=16 * 10**6, transcendentals=10**6),
    )(inputs, first_factor, second_factor, cotangent)


def solution(mesh):
    placed = (P("tok", "blk"), P("blk", "tok", None), P("blk", "tok", None), P("tok", "blk"))
    return jax.shard_map(
        body,
        mesh=mesh,
        in_specs=placed,
        out_specs=(P("tok", "blk"), P("blk", "tok", None), P("blk", "tok", None)),
        check_vma=False,
    )
```

time: 390 us -> 169 us (0.43)
  waiting for transfers between devices: 215 us -> 0 us
  Pallas kernels: 0 us -> 163 us
  matrix products: 58.6 us -> 0 us
  blocking collectives: 52 us -> 0 us
  local copies, waits for them, and re-layouts: 42.6 us -> 4.82 us
  between operations: 13.9 us -> 0.66 us
  starting transfers between devices: 6.81 us -> 0 us
    pallas_call x0 -> x1, Pallas kernels: none -> 163 us  [body(): pl.pallas_call(kernel, out_shape=(jax.ShapeDtypeStruct((count, width), F3...]
    reduce_scatter x2 -> x0, waiting for transfers between devices: 115 us -> none  [the longest x1 99.3 us: body(): lax.psum_scatter(first_grad, 'tok', scatter_dimension=1, tiled=True)]
    dot_general x6 -> x0, matrix products: 58.6 us -> none  [the longest x1 10.6 us: body(): jnp.einsum('tbo,bko->btk', delta_second, second_whole, precision=hp)]
    all_gather x2 -> x0, waiting for transfers between devices: 53.7 us -> none  [the longest x1 53.7 us: body(): lax.all_gather(first_factor, 'tok', axis=1, tiled=True)]
    all_to_all x1 -> x0, blocking collectives: 52 us -> none  [body(): lax.all_to_all(delta_mixed, 'blk', split_axis=2, concat_axis=0, tiled=True)]
    all_to_all x1 -> x0, waiting for transfers between devices: 45 us -> none  [body(): lax.all_to_all(first, 'blk', split_axis=0, concat_axis=2, tiled=True)]
    reshape x3 -> x0, local copies, waits for them, and re-layouts: 14.7 us -> none  [the longest x1 8.74 us: body(): jnp.einsum('tbi,stbg->bisg', xb, delta_view, precision=hp)]
    all_gather x1 -> x0, local copies, waits for them, and re-layouts: 8.72 us -> none  [body(): lax.all_gather(first_factor, 'tok', axis=1, tiled=True)]
  transfers between devices with their start and end apart: 5 -> 0, of which waited for: 4 -> 0; matrix products, arithmetic and copies ran while one was open for 20% -> 0% of each run, Pallas kernels for 0% -> 0%
where the time goes in v1:
time: 169 us; the launch traced here: 168 us
  Pallas kernels  163 us (96%)
  local copies, waits for them, and re-layouts  4.82 us (3%)
    pallas_call x1, Pallas kernels, body(): pl.pallas_call(kernel, out_shape=(jax.ShapeDtypeStruct((count, width), F3...  163 us
    unnamed x7, local copies, waits for them, and re-layouts  4.82 us

profile of v1, /device:TPU:1, one launch (start us, length us, event | category | flops | bytes accessed | tf_op | source)
XLA Modules:
  0.0 168.4 jit_solution(1058063580563537888)
XLA Ops:
  0.6 162.9 %shard_map.67 = (f32[256,2048]{1,0:T(8,128)}, f32[2,64,1024]{2,1,0:T(8,128)}, f32[2,64,1024]{2,1,0:T(8,128)}) custom-call(f32[256,2048]{1,0:T(8,128)} %x_hbm.1, f32[2,64,1024]{2,1,0:T(8,128)} %w1_hbm.1, f32[2,64,1024]{2,1,0:T(8,128)} %w2_hbm.1, f32[256,2048]{1,0:T(8,128)} %cot_hbm.1), custom_call_target="tpu_custom_call" | custom-call | flops 19000000512 | bytes 16000000 | tf_op jit(solution)/shard_map/pallas_call | solution.py:431
  163.6 0.0 copy-start.1
  163.6 0.0 copy-start
  163.6 3.2 %copy.10 = f32[256,2048]{1,0:T(8,128)} copy(f32[256,2048]{1,0:T(8,128)} %get-tuple-element.6) | data formatting | bytes 4194304
  166.8 0.0 copy-done.1
  166.8 0.8 copy.11
  167.6 0.0 copy-done
  167.6 0.8 copy.12
Async XLA Ops:
  163.6 3.2 %copy-start.1 = (f32[2,64,1024]{2,1,0:T(8,128)S(1)}, f32[2,64,1024]{2,1,0:T(8,128)}, u32[]{:S(2)}) copy-start(f32[2,64,1024]{2,1,0:T(8,128)} %get-tuple-element.7) | copy-start | bytes 1572868
  163.6 4.0 %copy-start = (f32[2,64,1024]{2,1,0:T(8,128)S(1)}, f32[2,64,1024]{2,1,0:T(8,128)}, u32[]{:S(2)}) copy-start(f32[2,64,1024]{2,1,0:T(8,128)} %get-tuple-element.8) | copy-start | bytes 1572868

commit v2 on v1

--- a/solution.py
+++ b/solution.py
@@ -14,6 +14,7 @@
 NT = (((1,), (1,)), ((), ()))
 AG_OVER_Y = (True, False)
 RS_OVER_Y = (True, False)
+CUTS = 2
 
 
 def halves(v):
@@ -91,67 +92,78 @@
     lax.fori_loop(0, 14, greet, 0)
     pl.semaphore_wait(barrier, 14 + len(near))
 
-    def ag(f, n, src, row, to):
-        return remote(src, wbuf.at[f, rows_at(row, slab)], ag_send.at[f, n], ag_recv.at[f, row], to)
-
-    def forward(f, n, row, to):
-        cp = ag(f, n, wbuf.at[f, rows_at(row, slab)], row, to)
-        cp.start()
+    cut = slab // CUTS
+
+    def piece(row, j):
+        return pl.ds(pl.multiple_of(row * slab + j * cut, cut), cut)
+
+    def ag(f, n, j, src, row, to):
+        return remote(src, wbuf.at[f, piece(row, j)], ag_send.at[f, n, j], ag_recv.at[f, row, j], to)
+
+    def forward(f, n, j, row, to):
+        ag(f, n, j, wbuf.at[f, piece(row, j)], row, to).start()
 
     def ag_first(f):
-        for h in range(2):
-            ag(f, h, w_hbm[f].at[h], t, tok(1, False, h)).start()
-            ag(f, 2 + h, w_hbm[f].at[h], t, tok(XS - 1, False, h)).start()
-            ag(f, 4 + h, w_hbm[f].at[h], t, tok(0, True, h)).start()
-        ag(f, 6, w_hbm[f].at[oc], t, tok(0, False, oc)).start()
-
-    def ag_wait(f, row):
-        ag(f, 0, wbuf.at[f, rows_at(row, slab)], row, tok(1, False, c)).wait_recv()
+        for j in range(CUTS):
+            part = pl.ds(j * cut, cut)
+            for h in range(2):
+                src = w_hbm[f].at[h, part]
+                ag(f, h, j, src, t, tok(1, False, h)).start()
+                ag(f, 2 + h, j, src, t, tok(XS - 1, False, h)).start()
+                ag(f, 4 + h, j, src, t, tok(0, True, h)).start()
+            ag(f, 6, j, w_hbm[f].at[oc, part], t, tok(0, False, oc)).start()
+
+    def ag_wait(f, row, j):
+        ag(f, 0, j, wbuf.at[f, piece(row, j)], row, tok(1, False, c)).wait_recv()
 
     def ag_second(f):
         low, high = slab_of(XS - 1, False, 0), slab_of(1, False, 1)
-        ag_wait(f, low)
-        forward(f, 7, low, tok(1, False, c))
-        ag_wait(f, high)
-        forward(f, 8, high, tok(XS - 1, False, c))
-        for h in range(2):
-            row = slab_of(0, True, h)
-            ag_wait(f, row)
-            forward(f, 9 + h, row, tok(1, False, c))
-            forward(f, 11 + h, row, tok(XS - 1, False, c))
+        for j in range(CUTS):
+            ag_wait(f, low, j)
+            forward(f, 7, j, low, tok(1, False, c))
+            ag_wait(f, high, j)
+            forward(f, 8, j, high, tok(XS - 1, False, c))
+            for h in range(2):
+                row = slab_of(0, True, h)
+                ag_wait(f, row, j)
+                forward(f, 9 + h, j, row, tok(1, False, c))
+                forward(f, 11 + h, j, row, tok(XS - 1, False, c))
 
     def ag_third(f):
-        if AG_OVER_Y[f]:
+        for j in range(CUTS):
+            if AG_OVER_Y[f]:
+                for h in range(2):
+                    row = slab_of(2, False, h)
+                    ag_wait(f, row, j)
+                    forward(f, 13 + h, j, row, tok(0, True, c))
+            else:
+                low, high = slab_of(XS - 1, True, 0), slab_of(1, True, 1)
+                ag_wait(f, low, j)
+                forward(f, 13, j, low, tok(1, False, c))
+                ag_wait(f, high, j)
+                forward(f, 14, j, high, tok(XS - 1, False, c))
+
+    def ag_rest(f):
+        for j in range(CUTS):
+            ag_wait(f, slab_of(0, False, oc), j)
+            ag_wait(f, slab_of(XS - 1, False, 1), j)
+            ag_wait(f, slab_of(1, False, 0), j)
+            if AG_OVER_Y[f]:
+                for h in range(2):
+                    ag_wait(f, slab_of(1, True, h), j)
+                    ag_wait(f, slab_of(XS - 1, True, h), j)
+            else:
+                for h in range(2):
+                    ag_wait(f, slab_of(2, False, h), j)
+                ag_wait(f, slab_of(XS - 1, True, 1), j)
+                ag_wait(f, slab_of(1, True, 0), j)
             for h in range(2):
-                row = slab_of(2, False, h)
-                ag_wait(f, row)
-                forward(f, 13 + h, row, tok(0, True, c))
-        else:
-            low, high = slab_of(XS - 1, True, 0), slab_of(1, True, 1)
-            ag_wait(f, low)
-            forward(f, 13, low, tok(1, False, c))
-            ag_wait(f, high)
-            forward(f, 14, high, tok(XS - 1, False, c))
-
-    def ag_rest(f):
-        ag_wait(f, slab_of(0, False, oc))
-        ag_wait(f, slab_of(XS - 1, False, 1))
-        ag_wait(f, slab_of(1, False, 0))
-        if AG_OVER_Y[f]:
-            for h in range(2):
-                ag_wait(f, slab_of(1, True, h))
-                ag_wait(f, slab_of(XS - 1, True, h))
-        else:
-            for h in range(2):
-                ag_wait(f, slab_of(2, False, h))
-            ag_wait(f, slab_of(XS - 1, True, 1))
-            ag_wait(f, slab_of(1, True, 0))
-        for h in range(2):
-            ag_wait(f, slab_of(2, True, h))
+                ag_wait(f, slab_of(2, True, h), j)
 
     def ag_sent(f):
-        for n in range(15):
-            ag(f, n, wbuf.at[f, rows_at(t, slab)], t, tok(1, False, c)).wait_send()
+        for j in range(CUTS):
+            for n in range(15):
+                ag(f, n, j, wbuf.at[f, piece(t, j)], t, tok(1, False, c)).wait_send()
 
     def split_factor(f):
         def step(i, _):
@@ -250,8 +262,6 @@
 
     ag_second(1)
     ag_third(1)
-    ag_rest(1)
-    split_factor(1)
     a2a_wait(0, ft, mt)
 
     def turn(src, keep):
@@ -270,6 +280,8 @@
         lax.fori_loop(0, order // 128, step, 0)
 
     turn(mt, True)
+    ag_rest(1)
+    split_factor(1)
 
     def second_step(i, _):
         at = rows_at(i, 256)
@@ -291,95 +303,94 @@
             a2a_start(1, dmt, d1t, 4 * q + r)
         return 0
 
-    lax.fori_loop(0, 4, mixed_step, 0)
-
-    def rs(f, slot, row, to):
+
+    def rs(f, slot, j, row, to):
         return remote(
-            wbuf.at[f, rows_at(row, slab)], rbuf.at[f, slot], rs_send.at[f, slot], rs_recv.at[f, slot], to
-        )
-
-    def rs_start(f, slot, row):
-        if slot in (1, 2, 3, 7, 8, 9) and not (RS_OVER_Y[f] and slot == 1):
+            wbuf.at[f, piece(row, j)], rbuf.at[f, slot, pl.ds(j * cut, cut)], rs_send.at[f, slot, j],
+            rs_recv.at[f, slot, j], to,
+        )
+
+    def rs_start(f, slot, j, row):
+        if slot >= 12 or (RS_OVER_Y[f] and slot < 2):
+            to = tok(0, True, c)
+        elif slot in (1, 2, 3, 7, 8, 9):
             to = tok(1, False, c)
-        elif slot in (0, 1, 12, 13) and (RS_OVER_Y[f] or slot >= 12):
-            to = tok(0, True, c)
         else:
             to = tok(XS - 1, False, c)
-        rs(f, slot, row, to).start()
-
-    def rs_add(f, row, slots):
+        rs(f, slot, j, row, to).start()
+
+    def rs_add(f, row, j, slots):
         for slot in slots:
-            rs(f, slot, t, tok(1, False, c)).wait_recv()
-        at = rows_at(row, slab)
-        total = rbuf[f, slots[0]]
+            rs(f, slot, j, t, tok(1, False, c)).wait_recv()
+        at = piece(row, j)
+        here = pl.ds(j * cut, cut)
+        total = rbuf[f, slots[0], here]
         for slot in slots[1:]:
-            total = total + rbuf[f, slot]
+            total = total + rbuf[f, slot, here]
         wbuf[f, at, :] = wbuf[f, at, :] + total
 
-    def gradient(f, lh, ll, rh, rl):
-        for dx in (2, 1, 3, 0):
-            at = rows_at((x + dx) % XS, 256)
-            wbuf[f, at, :] = product(lh[at, :], ll[at, :], rh[...], rl[...], NN)
-            if dx == 2:
-                if RS_OVER_Y[f]:
-                    rs_start(f, 0, slab_of(2, True, 0))
-                    rs_start(f, 1, slab_of(2, True, 1))
-                else:
-                    rs_start(f, 6, slab_of(2, False, 0))
-                    rs_start(f, 7, slab_of(2, False, 1))
-                    rs_start(f, 0, slab_of(2, True, 0))
-                    rs_start(f, 1, slab_of(2, True, 1))
-            elif dx == 1:
-                rs_start(f, 2, slab_of(1, True, 0))
-                if RS_OVER_Y[f]:
-                    rs_start(f, 3, slab_of(1, True, 1))
-                rs_start(f, 8, slab_of(1, False, 0))
-            elif dx == 3:
-                rs_start(f, 5, slab_of(3, True, 1))
-                if RS_OVER_Y[f]:
-                    rs_start(f, 4, slab_of(3, True, 0))
-                rs_start(f, 11, slab_of(3, False, 1))
+    def gradient(f, dx, lh, ll, rh, rl):
+        at = rows_at((x + dx) % XS, 256)
+        wbuf[f, at, :] = product(lh[at, :], ll[at, :], rh[...], rl[...], NN)
+        over_y = RS_OVER_Y[f]
+        if dx == 2:
+            sends = [(0, True, 0), (1, True, 1)]
+            if not over_y:
+                sends += [(6, False, 0), (7, False, 1)]
+        elif dx == 1:
+            sends = [(2, True, 0)] + ([(3, True, 1)] if over_y else []) + [(8, False, 0)]
+        elif dx == 3:
+            sends = [(5, True, 1)] + ([(4, True, 0)] if over_y else []) + [(11, False, 1)]
+        else:
+            sends = []
+        for slot, other, h in sends:
+            for j in range(CUTS):
+                rs_start(f, slot, j, slab_of(dx, other, h))
+
+    def rs_pass(f, j, row, slots, slot):
+        rs_add(f, row, j, slots)
+        rs_start(f, slot, j, row)
 
     def rs_middle(f):
+        cuts = range(CUTS)
         if RS_OVER_Y[f]:
-            for h in range(2):
-                row = slab_of(2, False, h)
-                rs_add(f, row, (h,))
-                rs_start(f, 6 + h, row)
+            for j in cuts:
+                for h in range(2):
+                    rs_pass(f, j, slab_of(2, False, h), (h,), 6 + h)
+            for j in cuts:
+                for h in range(2):
+                    rs_pass(f, j, slab_of(0, True, h), (2 + h, 4 + h), 12 + h)
+            for j in cuts:
+                rs_pass(f, j, slab_of(1, False, 1), (7,), 9)
+                rs_pass(f, j, slab_of(3, False, 0), (6,), 10)
         else:
-            row = slab_of(1, True, 1)
-            rs_add(f, row, (1,))
-            rs_start(f, 3, row)
-            row = slab_of(3, True, 0)
-            rs_add(f, row, (0,))
-            rs_start(f, 4, row)
-        row = slab_of(1, False, 1)
-        rs_add(f, row, (7,))
-        rs_start(f, 9, row)
-        row = slab_of(3, False, 0)
-        rs_add(f, row, (6,))
-        rs_start(f, 10, row)
-        for h in range(2):
-            row = slab_of(0, True, h)
-            rs_add(f, row, (2 + h, 4 + h))
-            rs_start(f, 12 + h, row)
+            for j in cuts:
+                rs_pass(f, j, slab_of(1, True, 1), (1,), 3)
+                rs_pass(f, j, slab_of(3, True, 0), (0,), 4)
+            for j in cuts:
+                rs_pass(f, j, slab_of(1, False, 1), (7,), 9)
+                rs_pass(f, j, slab_of(3, False, 0), (6,), 10)
+            for j in cuts:
+                for h in range(2):
+                    rs_pass(f, j, slab_of(0, True, h), (2 + h, 4 + h), 12 + h)
 
     def out_local(f):
         return pltpu.make_async_copy(wbuf.at[f, rows_at(t, slab)], g_hbm[f].at[c], loc_sem.at[f])
 
     def out_pair(f):
         return remote(
-            wbuf.at[f, rows_at(base + oc, slab)], g_hbm[f].at[c], rs_send.at[f, 14], rs_recv.at[f, 14], pair
+            wbuf.at[f, rows_at(base + oc, slab)], g_hbm[f].at[c], rs_send.at[f, 14, 0], rs_recv.at[f, 14, 0], pair
         )
 
     def out_wait(f):
         return remote(
-            wbuf.at[f, rows_at(base + oc, slab)], g_hbm[f].at[oc], rs_send.at[f, 14], rs_recv.at[f, 14], pair
+            wbuf.at[f, rows_at(base + oc, slab)], g_hbm[f].at[oc], rs_send.at[f, 14, 0], rs_recv.at[f, 14, 0], pair
         )
 
     def rs_end(f):
-        for h in range(2):
-            rs_add(f, slab_of(0, False, h), (8 + h, 10 + h, 12 + h))
+        for j in range(CUTS):
+            for h in range(2):
+                rs_add(f, slab_of(0, False, h), j, (8 + h, 10 + h, 12 + h))
         out_pair(f).start()
         out_local(f).start()
 
@@ -388,15 +399,20 @@
         out_pair(f).wait_send()
         out_wait(f).wait_recv()
         for slot in range(14):
-            rs(f, slot, t, tok(1, False, c)).wait_send()
+            for j in range(CUTS):
+                rs(f, slot, j, t, tok(1, False, c)).wait_send()
 
     ag_sent(1)
-    gradient(1, mth, mtl, d2h, d2l)
+    gradient(1, 2, mth, mtl, d2h, d2l)
+    lax.fori_loop(0, 4, mixed_step, 0)
+    for dx in (1, 3, 0):
+        gradient(1, dx, mth, mtl, d2h, d2l)
     rs_middle(1)
     a2a_wait(1, dmt, d1t)
     turn(d1t, False)
     ag_sent(0)
-    gradient(0, xth, xtl, ah, al)
+    for dx in (2, 1, 3, 0):
+        gradient(0, dx, xth, xtl, ah, al)
 
     def input_step(i, _):
         at = rows_at(i, 256)
@@ -421,6 +437,27 @@
     rs_done(0)
 
 
+def deliver(dx_in, g1_in, g2_in, dx_out, g1_out, g2_out, dx_held, g1_held, g2_held, in_sem, out_sem):
+    part = dx_in.shape[0] // 4
+    steps = [(dx_in, dx_held, dx_out, pl.ds(i * part, part)) for i in range(4)]
+    steps += [(g1_in, g1_held, g1_out, i) for i in range(2)]
+    steps += [(g2_in, g2_held, g2_out, i) for i in range(2)]
+    copies = [
+        (
+            pltpu.make_async_copy(src.at[at], held.at[at], in_sem.at[n]),
+            pltpu.make_async_copy(held.at[at], dst.at[at], out_sem.at[n]),
+        )
+        for n, (src, held, dst, at) in enumerate(steps)
+    ]
+    for first, _ in copies:
+        first.start()
+    for first, second in copies:
+        first.wait()
+        second.start()
+    for _, second in copies:
+        second.wait()
+
+
 def body(inputs, first_factor, second_factor, cotangent):
     count, width = inputs.shape
     blocks, slab, order = first_factor.shape
@@ -428,7 +465,7 @@
     wide = (chip, order)
     tall = (order, chip)
     dma = pltpu.SemaphoreType.DMA
-    return pl.pallas_call(
+    found = pl.pallas_call(
         kernel,
         out_shape=(
             jax.ShapeDtypeStruct((count, width), F32),
@@ -459,18 +496,26 @@
             dma((4,)),
             dma((3,)),
             dma((3,)),
-            dma((2, 15)),
+            dma((2, 15, CUTS)),
+            dma((2, 16, CUTS)),
             dma((2, 16)),
             dma((2, 16)),
-            dma((2, 16)),
-            dma((2, 15)),
-            dma((2, 15)),
+            dma((2, 15, CUTS)),
+            dma((2, 15, CUTS)),
         ],
         compiler_params=pltpu.CompilerParams(
             collective_id=0, has_side_effects=True, vmem_limit_bytes=60 * 1024 * 1024
         ),
         cost_estimate=pl.CostEstimate(flops=19 * 10**9, bytes_accessed=16 * 10**6, transcendentals=10**6),
     )(inputs, first_factor, second_factor, cotangent)
+    return pl.pallas_call(
+        deliver,
+        out_shape=tuple(jax.ShapeDtypeStruct(a.shape, F32) for a in found),
+        in_specs=[pl.BlockSpec(memory_space=pl.ANY)] * 3,
+        out_specs=[pl.BlockSpec(memory_space=pl.ANY)] * 3,
+        scratch_shapes=[pltpu.VMEM(a.shape, F32) for a in found] + [dma((8,)), dma((8,))],
+        cost_estimate=pl.CostEstimate(flops=0, bytes_accessed=6 * 10**6, transcendentals=0),
+    )(*found)
 
 
 def solution(mesh):

time: 169 us -> 155 us (0.917)
  Pallas kernels: 163 us -> 154 us
  local copies, waits for them, and re-layouts: 4.82 us -> 0 us
    pallas_call x1, Pallas kernels: 163 us -> 151 us  [body(): pl.pallas_call(kernel, out_shape=(jax.ShapeDtypeStruct((count, width), F3...]
    unnamed x7 -> x0, local copies, waits for them, and re-layouts: 4.82 us -> none
    pallas_call x0 -> x1, Pallas kernels: none -> 2.83 us  [body(): pl.pallas_call(deliver, out_shape=tuple((jax.ShapeDtypeStruct(a.shape, F3...]
where the time goes in v2:
time: 155 us
  Pallas kernels  154 us (99%)
    pallas_call x1, Pallas kernels, body(): pl.pallas_call(kernel, out_shape=(jax.ShapeDtypeStruct((count, width), F3...  151 us

profile of v2, /device:TPU:1, one launch (start us, length us, event | category | flops | bytes accessed | tf_op | source)
XLA Modules:
  0.0 154.7 jit_solution(15022996345174431381)
XLA Ops:
  0.6 151.2 %shard_map.67 = (f32[256,2048]{1,0:T(8,128)}, f32[2,64,1024]{2,1,0:T(8,128)}, f32[2,64,1024]{2,1,0:T(8,128)}) custom-call(f32[256,2048]{1,0:T(8,128)} %x_hbm.1, f32[2,64,1024]{2,1,0:T(8,128)} %w1_hbm.1, f32[2,64,1024]{2,1,0:T(8,128)} %w2_hbm.1, f32[256,2048]{1,0:T(8,128)} %cot_hbm.1), custom_call_target="tpu_custom_call" | custom-call | flops 19000000512 | bytes 16000000 | tf_op jit(solution)/shard_map/pallas_call | solution.py:468
  151.8 2.8 %shard_map.68 = (f32[256,2048]{1,0:T(8,128)}, f32[2,64,1024]{2,1,0:T(8,128)}, f32[2,64,1024]{2,1,0:T(8,128)}) custom-call(f32[256,2048]{1,0:T(8,128)} %get-tuple-element.6.dx_in, f32[2,64,1024]{2,1,0:T(8,128)} %get-tuple-element.7.g1_in, f32[2,64,1024]{2,1,0:T(8,128)} %get-tuple-element.8.g2_in), custom_call_target="tpu_custom_call" | custom-call | bytes 6000000 | tf_op jit(solution)/shard_map/pallas_call | solution.py:511

commit v3 on v2

v3 whole, which is shorter than its diff:
```python
import math

import jax
import jax.numpy as jnp
from jax import lax
from jax.experimental import pallas as pl
from jax.experimental.pallas import tpu as pltpu
from jax.sharding import PartitionSpec as P

F32 = jnp.float32
BF16 = jnp.bfloat16
XS = 4
NN = (((1,), (0,)), ((), ()))
NT = (((1,), (1,)), ((), ()))
AG_OVER_Y = (True, False)
RS_OVER_Y = (True, False)
CUTS = 2


def halves(v):
    high = v.astype(BF16)
    return high, (v - high.astype(F32)).astype(BF16)


def product(ah, al, bh, bl, dims):
    def dot(a, b):
        return lax.dot_general(a, b, dims, preferred_element_type=F32)

    return dot(ah, bh) + (dot(ah, bl) + dot(al, bh))


def rows_at(index, size):
    return pl.ds(pl.multiple_of(index * size, size), size)


def kernel(
    x_hbm, w1_hbm, w2_hbm, cot_hbm, dx_hbm, g1_hbm, g2_hbm,
    wbuf, gbuf, wh, wl, xs, cs, ah, al, xth, xtl, ft, mt, mth, mtl, d2h, d2l, dmt, d1t, rbuf,
    loc_sem, out_sem, pair_send, pair_recv, ag_send, ag_recv, a2a_send, a2a_recv, rs_send, rs_recv,
):
    w_hbm = (w1_hbm, w2_hbm)
    g_hbm = (g1_hbm, g2_hbm)
    k = lax.axis_index("blk")
    t = lax.axis_index("tok")
    x = t // 4
    y = (t // 2) % 2
    c = t % 2
    oc = 1 - c
    count = x_hbm.shape[0]
    slab = w1_hbm.shape[1]
    order = w1_hbm.shape[2]
    chip = 2 * count
    group = order // 16

    def tok(dx, other_y, core):
        yy = 1 - y if other_y else y
        return {"tok": ((x + dx) % XS) * 4 + yy * 2 + core}

    def slab_of(dx, other_y, core):
        return tok(dx, other_y, core)["tok"]

    def remote(src, dst, send, recv, to):
        return pltpu.make_async_remote_copy(
            src_ref=src, dst_ref=dst, send_sem=send, recv_sem=recv, device_id=to, device_id_type=pl.DeviceIdType.MESH
        )

    mine = rows_at(c, order)
    theirs = rows_at(oc, order)
    own = rows_at(c, count)
    local = [
        pltpu.make_async_copy(x_hbm.at[:, mine], xs.at[own], loc_sem.at[0]),
        pltpu.make_async_copy(cot_hbm.at[:, mine], cs.at[own], loc_sem.at[1]),
        pltpu.make_async_copy(w1_hbm.at[c], wbuf.at[0, rows_at(t, slab)], loc_sem.at[2]),
        pltpu.make_async_copy(w2_hbm.at[c], wbuf.at[1, rows_at(t, slab)], loc_sem.at[3]),
    ]
    for cp in local:
        cp.start()

    barrier = pltpu.get_barrier_semaphore()
    near = [tok(1, False, c), tok(-1 + XS, False, c), tok(0, True, c), tok(0, False, oc)]
    near += [tok(1, False, oc), tok(-1 + XS, False, oc), tok(0, True, oc)]
    for to in near:
        pl.semaphore_signal(barrier, inc=1, device_id=to, device_id_type=pl.DeviceIdType.MESH)

    def greet(i, _):
        kk = (k + 1 + i // 2) % 8
        pl.semaphore_signal(
            barrier, inc=1, device_id={"blk": kk, "tok": t - c + i % 2}, device_id_type=pl.DeviceIdType.MESH
        )
        return 0

    lax.fori_loop(0, 14, greet, 0)
    pl.semaphore_wait(barrier, 14 + len(near))

    z = k // 2
    near_half = z // 2
    wide = order // 2

    def half_of(f, j):
        if f == 0:
            return near_half if j else 1 - near_half
        return j

    def columns(f, j):
        return rows_at(half_of(f, j), wide)

    def ag(f, n, j, src, row, to):
        dst = wbuf.at[f, rows_at(row, slab), columns(f, j)]
        return remote(src, dst, ag_send.at[f, n, j], ag_recv.at[f, row, j], to)

    def forward(f, n, j, row, to):
        ag(f, n, j, wbuf.at[f, rows_at(row, slab), columns(f, j)], row, to).start()

    def ag_first(f, j):
        for h in range(2):
            src = w_hbm[f].at[h, :, columns(f, j)]
            ag(f, h, j, src, t, tok(1, False, h)).start()
            ag(f, 2 + h, j, src, t, tok(XS - 1, False, h)).start()
            ag(f, 4 + h, j, src, t, tok(0, True, h)).start()
        ag(f, 6, j, w_hbm[f].at[oc, :, columns(f, j)], t, tok(0, False, oc)).start()

    def ag_wait(f, row, j):
        ag(f, 0, j, wbuf.at[f, rows_at(row, slab), columns(f, j)], row, tok(1, False, c)).wait_recv()

    def ag_second(f, j):
        low, high = slab_of(XS - 1, False, 0), slab_of(1, False, 1)
        ag_wait(f, low, j)
        forward(f, 7, j, low, tok(1, False, c))
        ag_wait(f, high, j)
        forward(f, 8, j, high, tok(XS - 1, False, c))
        for h in range(2):
            row = slab_of(0, True, h)
            ag_wait(f, row, j)
            forward(f, 9 + h, j, row, tok(1, False, c))
            forward(f, 11 + h, j, row, tok(XS - 1, False, c))

    def ag_third(f, j):
        if AG_OVER_Y[f]:
            for h in range(2):
                row = slab_of(2, False, h)
                ag_wait(f, row, j)
                forward(f, 13 + h, j, row, tok(0, True, c))
        else:
            low, high = slab_of(XS - 1, True, 0), slab_of(1, True, 1)
            ag_wait(f, low, j)
            forward(f, 13, j, low, tok(1, False, c))
            ag_wait(f, high, j)
            forward(f, 14, j, high, tok(XS - 1, False, c))

    def ag_rest(f, j):
        ag_wait(f, slab_of(0, False, oc), j)
        ag_wait(f, slab_of(XS - 1, False, 1), j)
        ag_wait(f, slab_of(1, False, 0), j)
        if AG_OVER_Y[f]:
            for h in range(2):
                ag_wait(f, slab_of(1, True, h), j)
                ag_wait(f, slab_of(XS - 1, True, h), j)
        else:
            for h in range(2):
                ag_wait(f, slab_of(2, False, h), j)
            ag_wait(f, slab_of(XS - 1, True, 1), j)
            ag_wait(f, slab_of(1, True, 0), j)
        for h in range(2):
            ag_wait(f, slab_of(2, True, h), j)

    def ag_sent(f, j):
        for n in range(15):
            ag(f, n, j, wbuf.at[f, rows_at(t, slab), columns(f, j)], t, tok(1, False, c)).wait_send()

    def split_factor(f, j):
        across = columns(f, j)

        def step(i, _):
            at = rows_at(i, 128)
            high, low = halves(wbuf[f, at, across])
            wh[f, at, across] = high
            wl[f, at, across] = low
            return 0

        lax.fori_loop(0, order // 128, step, 0)

    ag_first(0, 0)
    ag_first(0, 1)
    pair = tok(0, False, oc)
    swap = [
        remote(x_hbm.at[:, theirs], xs.at[own], pair_send.at[0], pair_recv.at[0], pair),
        remote(cot_hbm.at[:, theirs], cs.at[own], pair_send.at[1], pair_recv.at[1], pair),
    ]
    for cp in swap:
        cp.start()
    for cp in local:
        cp.wait()
    for cp in swap:
        cp.wait()

    def split_x(i, _):
        at = rows_at(i, 128)
        high, low = halves(xs[:, at])
        ah[:, at] = high
        al[:, at] = low
        high, low = halves(xs[:, at].T)
        xth[at, :] = high
        xtl[at, :] = low
        return 0

    lax.fori_loop(0, order // 128, split_x, 0)

    me = 2 * k + c
    base = t - c

    def a2a(n, src, dst, s):
        return remote(
            src.at[rows_at(s, group)], dst.at[rows_at(me, group)], a2a_send.at[n, s], a2a_recv.at[n, me],
            {"blk": s // 2, "tok": base + s % 2},
        )

    def a2a_start(n, src, dst, s):
        @pl.when(s != me)
        def _():
            a2a(n, src, dst, s).start()

        @pl.when(s == me)
        def _():
            dst[rows_at(me, group), :] = src[rows_at(me, group), :]

    def a2a_wait(n, src, dst, half):
        def step(i, _):
            s = 8 * half + i

            @pl.when(s != me)
            def _():
                remote(
                    src.at[rows_at(s, group)], dst.at[rows_at(s, group)], a2a_send.at[n, s], a2a_recv.at[n, s],
                    {"blk": s // 2, "tok": base + s % 2},
                ).wait_recv()

            return 0

        lax.fori_loop(0, 8, step, 0)

    def a2a_sent(n, src, dst):
        def step(s, _):
            @pl.when(s != me)
            def _():
                a2a(n, src, dst, s).wait_send()

            return 0

        lax.fori_loop(0, 16, step, 0)

    def turn(src, half, keep):
        def step(i, _):
            at = rows_at(half * 4 + i, 128)
            v = src[at, :]
            if keep:
                high, low = halves(v)
                mth[at, :] = high
                mtl[at, :] = low
            high, low = halves(v.T)
            ah[:, at] = high
            al[:, at] = low
            return 0

        lax.fori_loop(0, 4, step, 0)

    def quarter(i):
        if i < 2:
            return 2 * (1 - near_half) + (z + i) % 2
        return 2 * near_half + (z + i + 1) % 2

    def first(j):
        for i in (2 * j, 2 * j + 1):
            q = quarter(i)
            at = rows_at(q, 256)
            part = product(ah[...], al[...], wh[0, :, at], wl[0, :, at], NN)
            ft[at, :] = part.T
            for r in range(4):
                a2a_start(0, ft, mt, 4 * q + r)

    def second(j):
        def step(i, _):
            at = rows_at(2 * j + i, 256)
            v = product(ah[...], al[...], wh[1, :, at], wl[1, :, at], NN)
            cdf = 0.5 * (1.0 + lax.erf(v * (1.0 / math.sqrt(2.0))))
            density = jnp.exp(-0.5 * v * v) * (1.0 / math.sqrt(2.0 * math.pi))
            high, low = halves(cs[:, at] * (cdf + v * density))
            d2h[:, at] = high
            d2l[:, at] = low
            return 0

        lax.fori_loop(0, 2, step, 0)

    def back():
        for i in range(4):
            q = quarter(i)
            at = rows_at(q, 256)
            dmt[at, :] = product(wh[1, at, :], wl[1, at, :], d2h[...], d2l[...], NT)
            for r in range(4):
                a2a_start(1, dmt, d1t, 4 * q + r)

    def rs(f, slot, j, row, to):
        return remote(
            gbuf.at[f, rows_at(row, slab), columns(f, j)], rbuf.at[f, slot, :, pl.ds(j * wide, wide)],
            rs_send.at[f, slot, j], rs_recv.at[f, slot, j], to,
        )

    def rs_start(f, slot, j, row):
        if slot >= 12 or (RS_OVER_Y[f] and slot < 2):
            to = tok(0, True, c)
        elif slot in (1, 2, 3, 7, 8, 9):
            to = tok(1, False, c)
        else:
            to = tok(XS - 1, False, c)
        rs(f, slot, j, row, to).start()

    def rs_add(f, row, j, slots):
        for slot in slots:
            rs(f, slot, j, t, tok(1, False, c)).wait_recv()
        at = rows_at(row, slab)
        across = columns(f, j)
        here = pl.ds(j * wide, wide)
        total = rbuf[f, slots[0], :, here]
        for slot in slots[1:]:
            total = total + rbuf[f, slot, :, here]
        gbuf[f, at, across] = gbuf[f, at, across] + total

    def gradient(f, j, dx, lh, ll, rh, rl):
        at = rows_at((x + dx) % XS, 256)
        across = columns(f, j)
        gbuf[f, at, across] = product(lh[at, :], ll[at, :], rh[:, across], rl[:, across], NN)
        over_y = RS_OVER_Y[f]
        if dx == 2:
            sends = [(0, True, 0), (1, True, 1)]
            if not over_y:
                sends += [(6, False, 0), (7, False, 1)]
        elif dx == 1:
            sends = [(2, True, 0)] + ([(3, True, 1)] if over_y else []) + [(8, False, 0)]
        elif dx == 3:
            sends = [(5, True, 1)] + ([(4, True, 0)] if over_y else []) + [(11, False, 1)]
        else:
            sends = []
        for slot, other, h in sends:
            rs_start(f, slot, j, slab_of(dx, other, h))

    def rs_pass(f, j, row, slots, slot):
        rs_add(f, row, j, slots)
        rs_start(f, slot, j, row)

    def rs_far(f, j):
        if RS_OVER_Y[f]:
            for h in range(2):
                rs_pass(f, j, slab_of(2, False, h), (h,), 6 + h)
        else:
            rs_pass(f, j, slab_of(1, True, 1), (1,), 3)
            rs_pass(f, j, slab_of(3, True, 0), (0,), 4)

    def rs_along(f, j):
        rs_pass(f, j, slab_of(1, False, 1), (7,), 9)
        rs_pass(f, j, slab_of(3, False, 0), (6,), 10)

    def rs_across(f, j):
        for h in range(2):
            rs_pass(f, j, slab_of(0, True, h), (2 + h, 4 + h), 12 + h)

    def out_local(f, j):
        across = columns(f, j)
        return pltpu.make_async_copy(
            gbuf.at[f, rows_at(t, slab), across], g_hbm[f].at[c, :, across], out_sem.at[f, j]
        )

    def out_pair(f, j, block):
        across = columns(f, j)
        return remote(
            gbuf.at[f, rows_at(base + oc, slab), across], g_hbm[f].at[block, :, across],
            rs_send.at[f, 14, j], rs_recv.at[f, 14, j], pair,
        )

    def rs_end(f, j):
        for h in range(2):
            rs_add(f, slab_of(0, False, h), j, (8 + h, 10 + h, 12 + h))
        out_pair(f, j, c).start()
        out_local(f, j).start()

    def rs_done(f, j):
        out_local(f, j).wait()
        out_pair(f, j, c).wait_send()
        out_pair(f, j, oc).wait_recv()
        for slot in range(14):
            rs(f, slot, j, t, tok(1, False, c)).wait_send()

    ag_second(0, 0)
    ag_third(0, 0)
    ag_second(0, 1)
    ag_first(1, 0)
    ag_rest(0, 0)
    split_factor(0, 0)
    first(0)
    ag_third(0, 1)
    ag_second(1, 0)
    ag_first(1, 1)
    ag_rest(0, 1)
    split_factor(0, 1)
    first(1)
    ag_third(1, 0)
    ag_second(1, 1)
    ag_rest(1, 0)
    split_factor(1, 0)
    for half in (1 - near_half, near_half):
        a2a_wait(0, ft, mt, half)
        turn(mt, half, True)
    ag_third(1, 1)
    second(0)
    for dx in (2, 1, 3, 0):
        gradient(1, 0, dx, mth, mtl, d2h, d2l)
    ag_rest(1, 1)
    split_factor(1, 1)
    second(1)
    gradient(1, 1, 2, mth, mtl, d2h, d2l)
    back()
    for dx in (1, 3, 0):
        gradient(1, 1, dx, mth, mtl, d2h, d2l)
    rs_far(1, 0)
    rs_along(1, 0)
    rs_far(1, 1)
    rs_along(1, 1)
    rs_across(1, 0)
    a2a_wait(1, dmt, d1t, 1 - near_half)
    turn(d1t, 1 - near_half, False)
    for dx in (2, 1, 3, 0):
        gradient(0, 0, dx, xth, xtl, ah, al)
    rs_across(1, 1)
    a2a_wait(1, dmt, d1t, near_half)
    turn(d1t, near_half, False)
    for dx in (2, 1, 3, 0):
        gradient(0, 1, dx, xth, xtl, ah, al)

    def input_step(i, _):
        at = rows_at(i, 256)
        xs[:, at] = product(ah[...], al[...], wh[0, at, :], wl[0, at, :], NT)
        return 0

    lax.fori_loop(0, 4, input_step, 0)
    dx_pair = remote(xs.at[rows_at(oc, count)], dx_hbm.at[:, mine], pair_send.at[2], pair_recv.at[2], pair)
    dx_wait = remote(xs.at[rows_at(oc, count)], dx_hbm.at[:, theirs], pair_send.at[2], pair_recv.at[2], pair)
    dx_local = pltpu.make_async_copy(xs.at[own], dx_hbm.at[:, mine], loc_sem.at[2])
    dx_pair.start()
    dx_local.start()
    rs_far(0, 0)
    rs_across(0, 0)
    rs_far(0, 1)
    rs_along(0, 0)
    rs_across(0, 1)
    rs_end(1, 0)
    rs_along(0, 1)
    rs_end(1, 1)
    rs_end(0, 0)
    rs_end(0, 1)
    dx_local.wait()
    dx_pair.wait_send()
    dx_wait.wait_recv()
    a2a_sent(0, ft, mt)
    a2a_sent(1, dmt, d1t)
    for f in range(2):
        for j in range(CUTS):
            ag_sent(f, j)
            rs_done(f, j)


def deliver(dx_in, g1_in, g2_in, dx_out, g1_out, g2_out, dx_held, g1_held, g2_held, in_sem, out_sem):
    part = dx_in.shape[0] // 4
    steps = [(dx_in, dx_held, dx_out, pl.ds(i * part, part)) for i in range(4)]
    steps += [(g1_in, g1_held, g1_out, i) for i in range(2)]
    steps += [(g2_in, g2_held, g2_out, i) for i in range(2)]
    copies = [
        (
            pltpu.make_async_copy(src.at[at], held.at[at], in_sem.at[n]),
            pltpu.make_async_copy(held.at[at], dst.at[at], out_sem.at[n]),
        )
        for n, (src, held, dst, at) in enumerate(steps)
    ]
    for first, _ in copies:
        first.start()
    for first, second in copies:
        first.wait()
        second.start()
    for _, second in copies:
        second.wait()


def body(inputs, first_factor, second_factor, cotangent):
    count, width = inputs.shape
    blocks, slab, order = first_factor.shape
    chip = 2 * count
    wide = (chip, order)
    tall = (order, chip)
    dma = pltpu.SemaphoreType.DMA
    found = pl.pallas_call(
        kernel,
        out_shape=(
            jax.ShapeDtypeStruct((count, width), F32),
            jax.ShapeDtypeStruct((blocks, slab, order), F32),
            jax.ShapeDtypeStruct((blocks, slab, order), F32),
        ),
        in_specs=[pl.BlockSpec(memory_space=pl.ANY)] * 4,
        out_specs=[pl.BlockSpec(memory_space=pl.ANY)] * 3,
        scratch_shapes=[
            pltpu.VMEM((2, order, order), F32),
            pltpu.VMEM((2, order, order), F32),
            pltpu.VMEM((2, order, order), BF16),
            pltpu.VMEM((2, order, order), BF16),
            pltpu.VMEM(wide, F32),
            pltpu.VMEM(wide, F32),
            pltpu.VMEM(wide, BF16),
            pltpu.VMEM(wide, BF16),
            pltpu.VMEM(tall, BF16),
            pltpu.VMEM(tall, BF16),
            pltpu.VMEM(tall, F32),
            pltpu.VMEM(tall, F32),
            pltpu.VMEM(tall, BF16),
            pltpu.VMEM(tall, BF16),
            pltpu.VMEM(wide, BF16),
            pltpu.VMEM(wide, BF16),
            pltpu.VMEM(tall, F32),
            pltpu.VMEM(tall, F32),
            pltpu.VMEM((2, 14, slab, order), F32),
            dma((4,)),
            dma((2, CUTS)),
            dma((3,)),
            dma((3,)),
            dma((2, 15, CUTS)),
            dma((2, 16, CUTS)),
            dma((2, 16)),
            dma((2, 16)),
            dma((2, 15, CUTS)),
            dma((2, 15, CUTS)),
        ],
        compiler_params=pltpu.CompilerParams(
            collective_id=0, has_side_effects=True, vmem_limit_bytes=60 * 1024 * 1024
        ),
        cost_estimate=pl.CostEstimate(flops=19 * 10**9, bytes_accessed=16 * 10**6, transcendentals=10**6),
    )(inputs, first_factor, second_factor, cotangent)
    return pl.pallas_call(
        deliver,
        out_shape=tuple(jax.ShapeDtypeStruct(a.shape, F32) for a in found),
        in_specs=[pl.BlockSpec(memory_space=pl.ANY)] * 3,
        out_specs=[pl.BlockSpec(memory_space=pl.ANY)] * 3,
        scratch_shapes=[pltpu.VMEM(a.shape, F32) for a in found] + [dma((8,)), dma((8,))],
        cost_estimate=pl.CostEstimate(flops=0, bytes_accessed=6 * 10**6, transcendentals=0),
    )(*found)


def solution(mesh):
    placed = (P("tok", "blk"), P("blk", "tok", None), P("blk", "tok", None), P("tok", "blk"))
    return jax.shard_map(
        body,
        mesh=mesh,
        in_specs=placed,
        out_specs=(P("tok", "blk"), P("blk", "tok", None), P("blk", "tok", None)),
        check_vma=False,
    )
```

time: 155 us -> 150 us (0.968)
  Pallas kernels: 154 us -> 149 us
    pallas_call x1, Pallas kernels: 151 us -> 146 us  [body(): pl.pallas_call(kernel, out_shape=(jax.ShapeDtypeStruct((count, width), F3...]
where the time goes in v3:
time: 150 us
  Pallas kernels  149 us (99%)
    pallas_call x1, Pallas kernels, body(): pl.pallas_call(kernel, out_shape=(jax.ShapeDtypeStruct((count, width), F3...  146 us

profile of v3, /device:TPU:1, one launch (start us, length us, event | category | flops | bytes accessed | tf_op | source)
XLA Modules:
  0.0 150.0 jit_solution(11283618180649974565)
XLA Ops:
  0.6 146.3 %shard_map.67 = (f32[256,2048]{1,0:T(8,128)}, f32[2,64,1024]{2,1,0:T(8,128)}, f32[2,64,1024]{2,1,0:T(8,128)}) custom-call(f32[256,2048]{1,0:T(8,128)} %x_hbm.1, f32[2,64,1024]{2,1,0:T(8,128)} %w1_hbm.1, f32[2,64,1024]{2,1,0:T(8,128)} %w2_hbm.1, f32[256,2048]{1,0:T(8,128)} %cot_hbm.1), custom_call_target="tpu_custom_call" | custom-call | flops 19000000512 | bytes 16000000 | tf_op jit(solution)/shard_map/pallas_call | solution.py:497
  147.0 2.8 %shard_map.68 = (f32[256,2048]{1,0:T(8,128)}, f32[2,64,1024]{2,1,0:T(8,128)}, f32[2,64,1024]{2,1,0:T(8,128)}) custom-call(f32[256,2048]{1,0:T(8,128)} %get-tuple-element.6.dx_in, f32[2,64,1024]{2,1,0:T(8,128)} %get-tuple-element.7.g1_in, f32[2,64,1024]{2,1,0:T(8,128)} %get-tuple-element.8.g2_in), custom_call_target="tpu_custom_call" | custom-call | bytes 6000000 | tf_op jit(solution)/shard_map/pallas_call | solution.py:542

commit v4 on v3

--- a/solution.py
+++ b/solution.py
@@ -12,7 +12,7 @@
 XS = 4
 NN = (((1,), (0,)), ((), ()))
 NT = (((1,), (1,)), ((), ()))
-AG_OVER_Y = (True, False)
+AG_OVER_Y = ((True, False), (False, False))
 RS_OVER_Y = (True, False)
 CUTS = 2
 
@@ -135,7 +135,7 @@
             forward(f, 11 + h, j, row, tok(XS - 1, False, c))
 
     def ag_third(f, j):
-        if AG_OVER_Y[f]:
+        if AG_OVER_Y[f][j]:
             for h in range(2):
                 row = slab_of(2, False, h)
                 ag_wait(f, row, j)
@@ -151,7 +151,7 @@
         ag_wait(f, slab_of(0, False, oc), j)
         ag_wait(f, slab_of(XS - 1, False, 1), j)
         ag_wait(f, slab_of(1, False, 0), j)
-        if AG_OVER_Y[f]:
+        if AG_OVER_Y[f][j]:
             for h in range(2):
                 ag_wait(f, slab_of(1, True, h), j)
                 ag_wait(f, slab_of(XS - 1, True, h), j)
@@ -179,18 +179,15 @@
 
         lax.fori_loop(0, order // 128, step, 0)
 
-    ag_first(0, 0)
-    ag_first(0, 1)
     pair = tok(0, False, oc)
     swap = [
         remote(x_hbm.at[:, theirs], xs.at[own], pair_send.at[0], pair_recv.at[0], pair),
         remote(cot_hbm.at[:, theirs], cs.at[own], pair_send.at[1], pair_recv.at[1], pair),
     ]
-    for cp in swap:
-        cp.start()
+    swap[0].start()
+    ag_first(0, 0)
+    ag_first(0, 1)
     for cp in local:
-        cp.wait()
-    for cp in swap:
         cp.wait()
 
     def split_x(i, _):
@@ -203,7 +200,6 @@
         xtl[at, :] = low
         return 0
 
-    lax.fori_loop(0, order // 128, split_x, 0)
 
     me = 2 * k + c
     base = t - c
@@ -298,20 +294,23 @@
             for r in range(4):
                 a2a_start(1, dmt, d1t, 4 * q + r)
 
-    def rs(f, slot, j, row, to):
+    def rs(f, slot, j, row, to, there=None):
+        there = slot if there is None else there
         return remote(
-            gbuf.at[f, rows_at(row, slab), columns(f, j)], rbuf.at[f, slot, :, pl.ds(j * wide, wide)],
-            rs_send.at[f, slot, j], rs_recv.at[f, slot, j], to,
+            gbuf.at[f, rows_at(row, slab), columns(f, j)], rbuf.at[f, there, :, pl.ds(j * wide, wide)],
+            rs_send.at[f, slot, j], rs_recv.at[f, there, j], to,
         )
 
     def rs_start(f, slot, j, row):
+        core = slot % 2 if slot >= 8 else c
+        there = slot - slot % 2 + c if slot >= 8 else slot
         if slot >= 12 or (RS_OVER_Y[f] and slot < 2):
-            to = tok(0, True, c)
+            to = tok(0, True, core)
         elif slot in (1, 2, 3, 7, 8, 9):
-            to = tok(1, False, c)
+            to = tok(1, False, core)
         else:
-            to = tok(XS - 1, False, c)
-        rs(f, slot, j, row, to).start()
+            to = tok(XS - 1, False, core)
+        rs(f, slot, j, row, to, there).start()
 
     def rs_add(f, row, j, slots):
         for slot in slots:
@@ -341,6 +340,8 @@
             sends = []
         for slot, other, h in sends:
             rs_start(f, slot, j, slab_of(dx, other, h))
+        if dx == 0:
+            rs(f, 14, j, slab_of(0, False, oc), pair).start()
 
     def rs_pass(f, j, row, slots, slot):
         rs_add(f, row, j, slots)
@@ -362,33 +363,42 @@
         for h in range(2):
             rs_pass(f, j, slab_of(0, True, h), (2 + h, 4 + h), 12 + h)
 
-    def out_local(f, j):
+    def out_own(f, j):
         across = columns(f, j)
         return pltpu.make_async_copy(
-            gbuf.at[f, rows_at(t, slab), across], g_hbm[f].at[c, :, across], out_sem.at[f, j]
-        )
-
-    def out_pair(f, j, block):
-        across = columns(f, j)
-        return remote(
-            gbuf.at[f, rows_at(base + oc, slab), across], g_hbm[f].at[block, :, across],
-            rs_send.at[f, 14, j], rs_recv.at[f, 14, j], pair,
+            gbuf.at[f, rows_at(t, slab), across], g_hbm[f].at[c, :, across], out_sem.at[f, j, 0]
+        )
+
+    def out_other(f, j):
+        return pltpu.make_async_copy(
+            rbuf.at[f, 14, :, pl.ds(j * wide, wide)], g_hbm[f].at[oc, :, columns(f, j)], out_sem.at[f, j, 1]
         )
 
     def rs_end(f, j):
-        for h in range(2):
-            rs_add(f, slab_of(0, False, h), j, (8 + h, 10 + h, 12 + h))
-        out_pair(f, j, c).start()
-        out_local(f, j).start()
+        rs_add(f, t, j, (8 + c, 10 + c, 12 + c))
+        out_own(f, j).start()
+        here = pl.ds(j * wide, wide)
+        slots = (14, 8 + oc, 10 + oc, 12 + oc)
+        for slot in slots:
+            rs(f, slot, j, t, pair).wait_recv()
+        total = rbuf[f, slots[0], :, here]
+        for slot in slots[1:]:
+            total = total + rbuf[f, slot, :, here]
+        rbuf[f, 14, :, here] = total
+        out_other(f, j).start()
 
     def rs_done(f, j):
-        out_local(f, j).wait()
-        out_pair(f, j, c).wait_send()
-        out_pair(f, j, oc).wait_recv()
-        for slot in range(14):
+        out_own(f, j).wait()
+        out_other(f, j).wait()
+
+    def rs_sent(f, j):
+        for slot in range(15):
             rs(f, slot, j, t, tok(1, False, c)).wait_send()
 
     ag_second(0, 0)
+    swap[1].start()
+    swap[0].wait()
+    lax.fori_loop(0, order // 128, split_x, 0)
     ag_third(0, 0)
     ag_second(0, 1)
     ag_first(1, 0)
@@ -409,16 +419,17 @@
         a2a_wait(0, ft, mt, half)
         turn(mt, half, True)
     ag_third(1, 1)
+    swap[1].wait()
     second(0)
-    for dx in (2, 1, 3, 0):
+    for dx in (2, 1, 3):
         gradient(1, 0, dx, mth, mtl, d2h, d2l)
     ag_rest(1, 1)
     split_factor(1, 1)
     second(1)
-    gradient(1, 1, 2, mth, mtl, d2h, d2l)
     back()
-    for dx in (1, 3, 0):
+    for dx in (2, 1, 3, 0):
         gradient(1, 1, dx, mth, mtl, d2h, d2l)
+    gradient(1, 0, 0, mth, mtl, d2h, d2l)
     rs_far(1, 0)
     rs_along(1, 0)
     rs_far(1, 1)
@@ -439,31 +450,40 @@
         xs[:, at] = product(ah[...], al[...], wh[0, at, :], wl[0, at, :], NT)
         return 0
 
-    lax.fori_loop(0, 4, input_step, 0)
+    rs_far(0, 0)
+    lax.fori_loop(0, 2, input_step, 0)
+    rs_across(0, 0)
+    rs_far(0, 1)
+    lax.fori_loop(2, 4, input_step, 0)
     dx_pair = remote(xs.at[rows_at(oc, count)], dx_hbm.at[:, mine], pair_send.at[2], pair_recv.at[2], pair)
     dx_wait = remote(xs.at[rows_at(oc, count)], dx_hbm.at[:, theirs], pair_send.at[2], pair_recv.at[2], pair)
     dx_local = pltpu.make_async_copy(xs.at[own], dx_hbm.at[:, mine], loc_sem.at[2])
     dx_pair.start()
     dx_local.start()
-    rs_far(0, 0)
-    rs_across(0, 0)
-    rs_far(0, 1)
     rs_along(0, 0)
     rs_across(0, 1)
     rs_end(1, 0)
-    rs_along(0, 1)
+    ag_sent(0, 0)
+    ag_sent(0, 1)
+    ag_sent(1, 0)
+    ag_sent(1, 1)
+    a2a_sent(0, ft, mt)
+    a2a_sent(1, dmt, d1t)
     rs_end(1, 1)
-    rs_end(0, 0)
-    rs_end(0, 1)
+    rs_sent(1, 0)
+    rs_sent(1, 1)
+    rs_done(1, 0)
     dx_local.wait()
     dx_pair.wait_send()
     dx_wait.wait_recv()
-    a2a_sent(0, ft, mt)
-    a2a_sent(1, dmt, d1t)
-    for f in range(2):
-        for j in range(CUTS):
-            ag_sent(f, j)
-            rs_done(f, j)
+    rs_along(0, 1)
+    rs_end(0, 0)
+    rs_done(1, 1)
+    rs_sent(0, 0)
+    rs_end(0, 1)
+    rs_sent(0, 1)
+    rs_done(0, 0)
+    rs_done(0, 1)
 
 
 def deliver(dx_in, g1_in, g2_in, dx_out, g1_out, g2_out, dx_held, g1_held, g2_held, in_sem, out_sem):
@@ -522,9 +542,9 @@
             pltpu.VMEM(wide, BF16),
             pltpu.VMEM(tall, F32),
             pltpu.VMEM(tall, F32),
-            pltpu.VMEM((2, 14, slab, order), F32),
+            pltpu.VMEM((2, 15, slab, order), F32),
             dma((4,)),
-            dma((2, CUTS)),
+            dma((2, CUTS, 2)),
             dma((3,)),
             dma((3,)),
             dma((2, 15, CUTS)),

time: 150 us -> 147 us (0.980)
  Pallas kernels: 149 us -> 146 us
    pallas_call x1, Pallas kernels: 146 us -> 143 us  [body(): pl.pallas_call(kernel, out_shape=(jax.ShapeDtypeStruct((count, width), F3...]
where the time goes in v4:
time: 147 us
  Pallas kernels  146 us (99%)
    pallas_call x1, Pallas kernels, body(): pl.pallas_call(kernel, out_shape=(jax.ShapeDtypeStruct((count, width), F3...  143 us

profile of v4, /device:TPU:1, one launch (start us, length us, event | category | flops | bytes accessed | tf_op | source)
XLA Modules:
  0.0 146.8 jit_solution(2563750774771872129)
XLA Ops:
  0.6 143.1 %shard_map.67 = (f32[256,2048]{1,0:T(8,128)}, f32[2,64,1024]{2,1,0:T(8,128)}, f32[2,64,1024]{2,1,0:T(8,128)}) custom-call(f32[256,2048]{1,0:T(8,128)} %x_hbm.1, f32[2,64,1024]{2,1,0:T(8,128)} %w1_hbm.1, f32[2,64,1024]{2,1,0:T(8,128)} %w2_hbm.1, f32[256,2048]{1,0:T(8,128)} %cot_hbm.1), custom_call_target="tpu_custom_call" | custom-call | flops 19000000512 | bytes 16000000 | tf_op jit(solution)/shard_map/pallas_call | solution.py:517
  143.8 2.8 %shard_map.68 = (f32[256,2048]{1,0:T(8,128)}, f32[2,64,1024]{2,1,0:T(8,128)}, f32[2,64,1024]{2,1,0:T(8,128)}) custom-call(f32[256,2048]{1,0:T(8,128)} %get-tuple-element.6.dx_in, f32[2,64,1024]{2,1,0:T(8,128)} %get-tuple-element.7.g1_in, f32[2,64,1024]{2,1,0:T(8,128)} %get-tuple-element.8.g2_in), custom_call_target="tpu_custom_call" | custom-call | bytes 6000000 | tf_op jit(solution)/shard_map/pallas_call | solution.py:562
